TPU v7x, 32 devices: a whole 2x2x4 slice. The times are simulated.
32 devices in a mesh: bx: 8 (over z, y), by: 4 (over x, core).
Axes of the slice: x: 2, y: 2, z: 4, core: 2. Of those that a mesh axis runs over, the one named last changes fastest.
Arguments:
- tracer: float32 [24, 1024, 512], P(None, 'bx', 'by'), may hold values from -6 to 6
- velocity: float32 [2, 24, 1024, 512], P(None, None, 'bx', 'by'), may hold values from -6 to 6
- vert_diff: float32 [24, 1024, 512], P(None, 'bx', 'by'), may hold values from 0.05 to 5
- vert_visc: float32 [24, 1024, 512], P(None, 'bx', 'by'), may hold values from 0.05 to 5
- surface_flux: float32 [1024, 512], P('bx', 'by'), may hold values from -6 to 6
- wind_stress: float32 [2, 1024, 512], P(None, 'bx', 'by'), may hold values from -6 to 6
- surface_coef: float32 [1024, 512], P('bx', 'by'), may hold values from 0.3 to 3
- height: float32 [4, 48, 16, 128], P('by', 'bx'), may hold values from -6 to 6
- block_land: int32 [64, 4], replicated, may hold values from 0 to 1, as said below
- tropic_position_table: int32 [64, 4], replicated, may hold values from -1 to 47, as said below
Outputs:
- tracer_new: float32 [24, 1024, 512], P(None, 'bx', 'by')
- velocity_new: float32 [2, 24, 1024, 512], P(None, None, 'bx', 'by')
- fresh_height: float32 [4, 48, 16, 128], P('by', 'bx')
Inputs may be any that keep to these rules, and one draw needn't show every extreme that they name: `block_land`: in each latitude row exactly 8 * (2) blocks are land. `tropic_position_table`: land blocks have -1; in each latitude row the ocean blocks hold the positions 0 to 47, each once, position p being slot p % 6 of longitude device p // 6. The ocean blocks that one longitude device holds in one row (blocks d * 8 to d * 8 + 7) go to different tropic devices.
All inputs are finite; a program needn't handle non-finite values.
Results may differ from a plain program's by a relative error of at most 0.000084.
Values sent between devices are 32-bit elements; how exact they have to be, the bound alone decides.
A program may use at most 128 MiB of HBM per device.

v0:
```python
import jax
import jax.numpy as jnp
from jax import lax
from jax.sharding import PartitionSpec as P

ITERS = 4


MIX_RATE = 0.2
DIV_SCALE = 0.1
GRAVITY_STEP = 0.5
SIDE_WEIGHT = 1.0
CORNER_WEIGHT = 0.5
LOW_BOUND = 0.04
HIGH_BOUND = 2.0


def padded_2(block, sides, width):
    for axis, dim in sides:
        count = lax.axis_size(axis)
        forward = [(i, i + 1) for i in range(count - 1)]
        forward.append((count - 1, 0))
        backward = [(target, source) for source, target in forward]
        low = lax.ppermute(
            lax.slice_in_dim(block, block.shape[dim] - width, None, axis=dim), axis, forward
        )
        high = lax.ppermute(lax.slice_in_dim(block, 0, width, axis=dim), axis, backward)
        block = jnp.concatenate([low, block, high], axis=dim)
    return block


def vertical_solve(rhs, coef, thickness):
    levels = rhs.shape[1]
    ratios = []
    values = []
    for level in range(levels):
        if level < levels - 1:
            upper = coef[:, level] / thickness[level]
        else:
            upper = jnp.zeros_like(rhs[:, level])
        if level > 0:
            lower = coef[:, level - 1] / thickness[level]
        else:
            lower = jnp.zeros_like(rhs[:, level])
        centre = 1.0 + upper + lower
        if level == 0:
            denom = centre
            value = rhs[:, level] / denom
        else:
            denom = centre + lower * ratios[-1]
            value = (rhs[:, level] + lower * values[-1]) / denom
        ratios.append(-upper / denom)
        values.append(value)
    answer = [values[-1]]
    for level in range(levels - 2, -1, -1):
        answer.append(values[level] - ratios[level] * answer[-1])
    return jnp.stack(answer[::-1], axis=1)


def chebyshev(start, source, diagonal, operator):
    scale_a = 2.0 / (HIGH_BOUND - LOW_BOUND)
    gamma = (HIGH_BOUND + LOW_BOUND) / 2.0
    result = start
    residual = source - operator(result)
    update = residual / (gamma * diagonal)
    result = result + update
    weight = 2.0 / gamma
    for step in range(1, ITERS):
        residual = source - operator(result)
        weight = 1.0 / (gamma - weight / (4.0 * scale_a * scale_a))
        update = weight * residual / diagonal + (gamma * weight - 1.0) * update
        result = result + update
    return result


def horizontal_mix(padded, ocean_rim):
    size_x = padded.shape[-2]
    size_y = padded.shape[-1]
    centre = padded[..., 1:-1, 1:-1]
    total = jnp.zeros_like(centre)
    for step_x, step_y in ((1, 0), (-1, 0), (0, 1), (0, -1)):
        near = padded[..., 1 + step_x : size_x - 1 + step_x, 1 + step_y : size_y - 1 + step_y]
        weight = ocean_rim[1 + step_x : size_x - 1 + step_x, 1 + step_y : size_y - 1 + step_y]
        total = total + weight * (near - centre)
    return ocean_rim[1:-1, 1:-1] * total


def nine_point(padded, field, diagonal, ocean):
    sides = (
        padded[..., 2:, 1:-1]
        + padded[..., :-2, 1:-1]
        + (padded[..., 1:-1, 2:] + padded[..., 1:-1, :-2])
    )
    corners = (
        padded[..., 2:, 2:] + padded[..., :-2, 2:] + (padded[..., 2:, :-2] + padded[..., :-2, :-2])
    )
    return ocean * (diagonal * field - SIDE_WEIGHT * sides - CORNER_WEIGHT * corners)


def shards(
    tracer,
    velocity,
    vert_diff,
    vert_visc,
    surface_flux,
    wind_stress,
    surface_coef,
    height,
    block_land,
    tropic_position_table,
):
    lon_count = lax.axis_size("bx")
    lat_count = lax.axis_size("by")
    lon_index = lax.axis_index("bx")
    lat_index = lax.axis_index("by")
    levels, width_x, width_y = tracer.shape
    slots = height.shape[1]
    block_len = height.shape[2]
    blocks = width_x // block_len
    total_blocks = block_land.shape[0]
    ocean_table = (1 - block_land).astype(jnp.float32)
    padded_table = jnp.pad(ocean_table, ((0, 0), (1, 1)))
    near_rows = lax.dynamic_slice_in_dim(padded_table, lat_index, 3, axis=1)
    block_ids = (lon_index * blocks - 1 + jnp.arange(blocks + 2)) % total_blocks
    picker = (block_ids[:, None] == jnp.arange(total_blocks)[None, :]).astype(jnp.float32)
    near_blocks = jnp.dot(picker, near_rows, precision=lax.Precision.HIGHEST)
    along_x = jnp.concatenate(
        [near_blocks[:1], jnp.repeat(near_blocks[1:-1], block_len, axis=0), near_blocks[-1:]],
        axis=0,
    )
    lat_cells = jnp.arange(width_y + 2)
    lat_select = jnp.stack(
        [lat_cells == 0, (lat_cells > 0) & (lat_cells <= width_y), lat_cells == width_y + 1]
    ).astype(jnp.float32)
    ocean_rim = jnp.dot(along_x, lat_select, precision=lax.Precision.HIGHEST)
    ocean_cells = ocean_rim[1:-1, 1:-1]
    thickness = 1.0 + jnp.arange(levels, dtype=jnp.float32) / levels
    fields = jnp.concatenate([tracer[None], velocity], axis=0)
    fields_rim = padded_2(fields, (("bx", 2), ("by", 3)), 1) * ocean_rim
    transport_rim = jnp.sum(thickness[:, None, None] * fields_rim[1:], axis=1)
    divergence = ocean_cells * (
        0.5
        * (
            transport_rim[0, 2:, 1:-1]
            - transport_rim[0, :-2, 1:-1]
            + (transport_rim[1, 1:-1, 2:] - transport_rim[1, 1:-1, :-2])
        )
    )
    map_row = lax.dynamic_index_in_dim(tropic_position_table, lat_index, axis=1, keepdims=False)
    map_grid = map_row.reshape(lon_count, blocks)
    own_positions = lax.dynamic_slice_in_dim(map_row, lon_index * blocks, blocks)
    own_targets = jnp.where(own_positions >= 0, own_positions // slots, -1)
    send_pick = (own_targets[None, :] == jnp.arange(lon_count)[:, None]).astype(jnp.float32)
    wanted = lon_index * slots + jnp.arange(slots)
    hits = (map_grid[None, :, :] == wanted[:, None, None]).astype(jnp.int32)
    slot_pick = jnp.sum(hits, axis=2).astype(jnp.float32)
    block_number = jnp.arange(lon_count)[:, None] * blocks + jnp.arange(blocks)[None, :]
    own_block = jnp.sum(hits * block_number[None], axis=(1, 2))
    stacked = jnp.stack([divergence, surface_coef])
    pieces = stacked.reshape(stacked.shape[0], blocks, block_len, width_y)
    outgoing = jnp.einsum("tj,fjxy->tfxy", send_pick, pieces, precision=lax.Precision.HIGHEST)
    arrived = lax.all_to_all(outgoing, "bx", split_axis=0, concat_axis=0, tiled=True)
    moved = jnp.einsum("sn,nfxy->fsxy", slot_pick, arrived, precision=lax.Precision.HIGHEST)
    start = height[0]
    source = moved[1] * start - DIV_SCALE * moved[0]
    diagonal = moved[1] + 6.0
    edge_len = 2 * width_y + 2 * block_len
    index_pieces_list = []
    inside_parts = []
    for shift_x, shift_y in ((-1, 0), (1, 0), (0, 1), (0, -1), (-1, 1), (1, 1), (-1, -1), (1, -1)):
        target_block = (own_block + shift_x) % total_blocks
        target_row = lat_index + shift_y
        row_clip = jnp.clip(target_row, 0, lat_count - 1)
        target_pos = tropic_position_table[target_block, row_clip]
        inside = (target_row >= 0) & (target_row < lat_count) & (target_pos >= 0)
        inside_parts.append(inside.astype(jnp.float32))
        safe_pos = jnp.maximum(target_pos, 0)
        holder = safe_pos // slots
        target_slot = safe_pos % slots
        index_pieces_list.append((holder * lat_count + row_clip) * slots + target_slot)
    index_all = jnp.concatenate(index_pieces_list)
    inside_all = jnp.stack(inside_parts)

    def operator(field):
        edges = jnp.concatenate(
            [field[:, 0, :], field[:, -1, :], field[:, :, 0], field[:, :, -1]], axis=1
        )
        table = lax.all_gather(edges[None], ("bx", "by"), axis=0, tiled=True).reshape(-1, edge_len)
        picked = table[index_all].reshape(8, slots, edge_len) * inside_all[:, :, None]
        west_edge = picked[0][:, width_y : 2 * width_y]
        east_edge = picked[1][:, :width_y]
        north_edge = picked[2][:, 2 * width_y : 2 * width_y + block_len]
        south_edge = picked[3][:, 2 * width_y + block_len :]
        north_west = picked[4][:, width_y]
        north_east = picked[5][:, 0]
        south_west = picked[6][:, 2 * width_y - 1]
        south_east = picked[7][:, width_y - 1]
        middle = jnp.concatenate([south_edge[:, :, None], field, north_edge[:, :, None]], axis=2)
        left_line = jnp.concatenate([south_west[:, None], west_edge, north_west[:, None]], axis=1)[
            :, None, :
        ]
        right_line = jnp.concatenate([south_east[:, None], east_edge, north_east[:, None]], axis=1)[
            :, None, :
        ]
        padded = jnp.concatenate([left_line, middle, right_line], axis=1)
        return nine_point(padded, field, diagonal, 1.0)

    surface_slots = chebyshev(start, source, diagonal, operator)
    fresh_height = surface_slots[None]
    outgoing = jnp.einsum("sn,fsxy->nfxy", slot_pick, fresh_height, precision=lax.Precision.HIGHEST)
    arrived = lax.all_to_all(outgoing, "bx", split_axis=0, concat_axis=0, tiled=True)
    pieces = jnp.einsum("tj,tfxy->fjxy", send_pick, arrived, precision=lax.Precision.HIGHEST)
    surface = pieces.reshape(fresh_height.shape[0], width_x, width_y)[0]
    mixed = fields + MIX_RATE * horizontal_mix(fields_rim, ocean_rim)
    rhs = mixed.at[:, 0].add(
        jnp.concatenate([surface_flux[None], wind_stress], axis=0) / thickness[0]
    )
    coef = jnp.stack([vert_diff, vert_visc, vert_visc])
    solved = vertical_solve(rhs, coef, thickness) * ocean_cells
    surface_rim = padded_2(surface, (("bx", 0), ("by", 1)), 1) * ocean_rim
    grad_x = 0.5 * (surface_rim[2:, 1:-1] - surface_rim[:-2, 1:-1])
    grad_y = 0.5 * (surface_rim[1:-1, 2:] - surface_rim[1:-1, :-2])
    velocity_new = ocean_cells * (solved[1:] - GRAVITY_STEP * jnp.stack([grad_x, grad_y])[:, None])
    tracer_new = solved[0]
    return (tracer_new, velocity_new, fresh_height)


def solution(mesh):
    placed = (
        P(None, "bx", "by"),
        P(None, None, "bx", "by"),
        P(None, "bx", "by"),
        P(None, "bx", "by"),
        P("bx", "by"),
        P(None, "bx", "by"),
        P("bx", "by"),
        P("by", "bx", None, None),
        P(),
        P(),
    )
    return jax.shard_map(
        shards,
        mesh=mesh,
        in_specs=placed,
        out_specs=(P(None, "bx", "by"), P(None, None, "bx", "by"), P("by", "bx", None, None)),
        check_vma=False,
    )
```

profile of v0, /device:TPU:1, one launch (start us, length us, event | category | flops | bytes accessed | tf_op | source)
XLA Modules:
  0.0 353.5 jit_solution(9705799707729977806)
XLA Ops:
  0.7 1.8 fusion.93
  2.5 5.1 %collective-permute-start.1 = (f32[3,24,1,128]{3,1,2,0:T(8,128)}, f32[3,24,1,128]{3,1,2,0:T(8,128)}, u32[]{:S(2)}, u32[]{:S(2)}) collective-permute-start(f32[3,24,1,128]{3,1,2,0:T(8,128)} %bitcast.3), channel_id=1, source_target_pairs={{4,0},{8,4},{12,8},{16,12},{20,16},{24,20},{28,24},{0,28},{5,1},{9... | collective-permute-start | bytes 110600 | tf_op jit(solution)/shard_map/ppermute | solution.py:27
  9.9 1.0 fusion.96
  19.3 43.8 %all-gather.4 = f32[32,6,288]{2,1,0:T(8,128)S(1)} all-gather(f32[1,6,288]{2,1,0:T(8,128)S(1)} %maximum_bitcast_fusion), channel_id=2, replica_groups=mesh['bx'=8,'by'=4] {'bx','by'}, dimensions={0}, use_global_device_ids=true | all-gather | bytes 228096 | tf_op jit(solution)/shard_map/all_gather | solution.py:188
  65.5 18.5 %negate_divide_fusion.3 = (f32[3,1,128,128]{3,2,1,0:T(8,128)}, f32[3,1,128,128]{3,2,1,0:T(8,128)}, f32[3,1,128,128]{3,2,1,0:T(8,128)S(1)}, f32[3,1,128,128]{3,2,...) fusion(f32[]{:T(128)} %bitcast.28, ...), kind=kLoop, calls=%fused_computation.144 | loop fusion | flops 9633792 | bytes 10616912 | tf_op jit(solution)/shard_map/div | solution.py:52
  84.5 2.1 pad_maximum_fusion.1
  86.6 5.5 %fusion.179 = (f32[3,24,130,1]{3,2,1,0:T(8,128)}, f32[3,24,130,1]{3,2,1,0:T(8,128)}) fusion(f32[3,24,130,128]{3,2,1,0:T(8,128)S(1)} %pad_maximum_fusion.1), kind=kLoop, calls=%fused_computation.537 | loop fusion | bytes 149760 | tf_op jit(solution)/shard_map/slice | solution.py:25
  92.2 5.3 %copy.284 = f32[3,24,130,1]{2,1,3,0:T(8,128)} copy(f32[3,24,130,1]{3,2,1,0:T(8,128)} %get-tuple-element.120) | data formatting | bytes 74880 | tf_op jit(solution)/shard_map/slice | solution.py:25
  97.4 5.3 %copy.285 = f32[3,24,130,1]{2,1,3,0:T(8,128)} copy(f32[3,24,130,1]{3,2,1,0:T(8,128)} %get-tuple-element.121) | data formatting | bytes 74880 | tf_op jit(solution)/shard_map/slice | solution.py:27
  102.9 1.6 collective-permute-start.2
  105.1 1.5 copy.295
  106.6 4.3 %copy.286 = f32[3,24,130,1]{3,2,1,0:T(8,128)} copy(f32[3,24,130,1]{2,1,3,0:T(8,128)} %collective-permute-done.2) | data formatting | bytes 74880 | tf_op jit(solution)/shard_map/ppermute | solution.py:24
  110.9 4.3 %copy.287 = f32[3,24,130,1]{3,2,1,0:T(8,128)} copy(f32[3,24,130,1]{2,1,3,0:T(8,128)} %collective-permute-done.3) | data formatting | bytes 74880 | tf_op jit(solution)/shard_map/ppermute | solution.py:27
  115.1 8.9 %maximum_multiply_fusion = f32[3,24,130,130]{3,2,1,0:T(8,128)S(1)} fusion(f32[3,24,130,1]{3,2,1,0:T(8,128)} %copy.287, f32[3,24,1,128]{3,2,1,0:T(1,128)} %bitcast.4, f32[2,24,128,128]{3,2,1,0:T(8,128)S(1)} %copy-done.2, f32[1,24,128,128]{3,2,1,0:T(8,128)} %bitcast.320, f32[3,24,1,128]{3,2,1,0:T(1,128)} %bitcast.2, f32[3,24,130,1]{3,2,1,0:T(8,128)} %copy.286, ...), kind=kLoop, calls=%fused_computation.12 | loop fusion | flops 7300800 | bytes 9802000 | tf_op jit(solution)/shard_map/mul | solution.py:139
  124.1 3.9 %copy-done.1 = f32[3,24,130,130]{3,2,1,0:T(8,128)} copy-done((f32[3,24,130,130]{3,2,1,0:T(8,128)}, f32[3,24,130,130]{3,2,1,0:T(8,128)S(1)}, u32[]{:S(2)}) %copy-start.1) | copy-done | bytes 4867224
  130.5 4.2 %all-to-all-start = ((f32[8,2,16,128]{3,2,1,0:T(8,128)}), f32[8,2,16,128]{3,2,1,0:T(8,128)}, u32[]{:S(2)}, u32[]{:S(2)}) async-start(f32[8,2,16,128]{3,2,1,0:T(8,128)} %copy.297), calls=%async_computation | async-start | bytes 262144 | tf_op jit(solution)/shard_map/all_to_all | solution.py:162
  134.7 19.7 %fusion.1 = f32[3,24,128,128]{3,2,1,0:T(8,128)} fusion(f32[2,24,128,128]{3,2,1,0:T(8,128)S(1)} %copy-done.2, f32[1,24,128,128]{3,2,1,0:T(8,128)} %bitcast.321, f32[3,24,130,130]{3,2,1,0:T(8,128)} %copy-done.1, f32[128,128]{1,0:T(8,128)} %get-tuple-element.135, f32[128,128]{1,0:T(8,128)} %get-tuple-element.136, f32[128,128]{1,0:T(8,128)} %get-tuple-element.137, ...), kind=kLoop, calls=%fused_computation.21 | loop fusion | flops 17694720 | bytes 33357824 | tf_op jit(solution)/shard_map/add | solution.py:214
  154.7 19.0 %fusion.16 = (f32[3,1,128,128]{3,2,1,0:T(8,128)S(1)}, f32[3,1,128,128]{3,2,1,0:T(8,128)S(1)}, f32[3,1,128,128]{3,2,1,0:T(8,128)S(1)}, f32[3,1,128,128]{3,2,1,0:T...) fusion(f32[3,24,128,128]{3,2,1,0:T(8,128)} %fusion.1, ...), kind=kLoop, calls=%fused_computation.56 | loop fusion | flops 8896512 | bytes 15138896 | tf_op jit(solution)/shard_map/div | solution.py:51
  174.0 7.0 %subtract_dynamic-update-slice_fusion = (f32[3,24,128,128]{3,2,1,0:T(8,128)}, f32[3,1,128,128]{3,2,1,0:T(8,128)S(1)}, f32[3,1,128,128]{3,2,1,0:T(8,128)S(1)}, f3...) fusion(f32[3,1,128,128]{3,2,1,0:T(8,128)S(1)} %copy-done.23, ...), kind=kLoop, calls=%fused_computation.115 | loop fusion | flops 5308415 | bytes 15728664
  196.1 3.1 constant_dynamic-update-slice_fusion.1
  199.3 1.2 convolution_bitcast_fusion
  201.2 43.5 %all-gather.5 = f32[32,6,288]{2,1,0:T(8,128)S(1)} all-gather(f32[1,6,288]{2,1,0:T(8,128)S(1)} %maximum_bitcast_fusion.1), channel_id=3, replica_groups=mesh['bx'=8,'by'=4] {'bx','by'}, dimensions={0}, use_global_device_ids=true | all-gather | bytes 228096 | tf_op jit(solution)/shard_map/all_gather | solution.py:188
  247.1 37.8 %all-gather.6 = f32[32,6,288]{2,1,0:T(8,128)S(1)} all-gather(f32[1,6,288]{2,1,0:T(8,128)S(1)} %maximum_bitcast_fusion.2), channel_id=4, replica_groups=mesh['bx'=8,'by'=4] {'bx','by'}, dimensions={0}, use_global_device_ids=true | all-gather | bytes 228096 | tf_op jit(solution)/shard_map/all_gather | solution.py:188
  287.2 39.0 %all-gather.7 = f32[32,6,288]{2,1,0:T(8,128)S(1)} all-gather(f32[1,6,288]{2,1,0:T(8,128)S(1)} %maximum_bitcast_fusion.3), channel_id=5, replica_groups=mesh['bx'=8,'by'=4] {'bx','by'}, dimensions={0}, use_global_device_ids=true | all-gather | bytes 228096 | tf_op jit(solution)/shard_map/all_gather | solution.py:188
  329.1 3.4 all-to-all-start.1
  333.2 5.0 %all-to-all-done.1 = f32[8,1,16,128]{3,2,1,0:T(8,128)S(1)} async-done(((f32[8,1,16,128]{3,2,1,0:T(8,128)}), f32[8,1,16,128]{3,2,1,0:T(8,128)S(1)}, u32[]{:S(2)}, u32[]{:S(2)}) %all-to-all-start.1) | async-done | bytes 65568 | tf_op jit(solution)/shard_map/all_to_all | solution.py:211
  338.6 4.1 %collective-permute-start.5 = (f32[1,128]{1,0:T(1,128)S(1)}, f32[1,128]{1,0:T(1,128)S(1)}, u32[]{:S(2)}, u32[]{:S(2)}) collective-permute-start(f32[1,128]{1,0:T(1,128)S(1)} %get-tuple-element.175), channel_id=1, source_target_pairs={{4,0},{8,4},{12,8},{16,12},{20,16},{24,20},{28,24},{0,28},{5,1},{9... | collective-permute-start | bytes 1544 | tf_op jit(solution)/shard_map/ppermute | solution.py:27
  342.7 2.7 broadcast_multiply_fusion
  345.5 1.9 collective-permute-start.6
  347.5 1.2 slice_bitcast_fusion
  349.4 1.8 collective-permute-done.7
  351.5 2.0 fusion.11
  (287 shorter events, 42.2 us)
Async XLA Ops:
  2.5 82.0 %collective-permute-start.1 = (f32[3,24,1,128]{3,1,2,0:T(8,128)}, f32[3,24,1,128]{3,1,2,0:T(8,128)}, u32[]{:S(2)}, u32[]{:S(2)}) collective-permute-start(f32[3,24,1,128]{3,1,2,0:T(8,128)} %bitcast.3), channel_id=1, source_target_pairs={{4,0},{8,4},{12,8},{16,12},{20,16},{24,20},{28,24},{0,28},{5,1},{9... | collective-permute-start | bytes 110600 | tf_op jit(solution)/shard_map/ppermute | solution.py:27
  7.6 76.9 %collective-permute-start = (f32[3,24,1,128]{3,1,2,0:T(8,128)}, f32[3,24,1,128]{3,1,2,0:T(8,128)}, u32[]{:S(2)}, u32[]{:S(2)}) collective-permute-start(f32[3,24,1,128]{3,1,2,0:T(8,128)} %bitcast.1), channel_id=1, source_target_pairs={{0,4},{4,8},{8,12},{12,16},{16,20},{20,24},{24,28},{28,0},{1,5},{5... | collective-permute-start | bytes 110600 | tf_op jit(solution)/shard_map/ppermute | solution.py:24
  18.2 47.2 %copy-start.37 = (f32[8,6]{1,0:T(8,128)}, f32[8,6]{1,0:T(8,128)S(1)}, u32[]{:S(2)}) copy-start(f32[8,6]{1,0:T(8,128)S(1)} %stack.36) | copy-start | bytes 580
  18.3 47.2 %copy-start.40 = (s32[1024]{0:T(1024)}, s32[1024]{0:T(1024)S(1)}, u32[]{:S(2)}) copy-start(s32[1024]{0:T(1024)S(1)} %pad_clamp_fusion) | copy-start | bytes 12292
  102.7 8.1 %collective-permute-start.3 = (f32[3,24,130,1]{2,1,3,0:T(8,128)}, f32[3,24,130,1]{2,1,3,0:T(8,128)}, u32[]{:S(2)}, u32[]{:S(2)}) collective-permute-start(f32[3,24,130,1]{2,1,3,0:T(8,128)} %copy.285), channel_id=1, source_target_pairs={{1,0},{2,1},{3,2},{0,3},{5,4},{6,5},{7,6},{4,7},{9,8},{10,9},{11,1... | collective-permute-start | bytes 112328 | tf_op jit(solution)/shard_map/ppermute | solution.py:27
  102.9 3.7 %collective-permute-start.2 = (f32[3,24,130,1]{2,1,3,0:T(8,128)}, f32[3,24,130,1]{2,1,3,0:T(8,128)}, u32[]{:S(2)}, u32[]{:S(2)}) collective-permute-start(f32[3,24,130,1]{2,1,3,0:T(8,128)} %copy.284), channel_id=1, source_target_pairs={{0,1},{1,2},{2,3},{3,0},{4,5},{5,6},{6,7},{7,4},{8,9},{9,10},{10,1... | collective-permute-start | bytes 112328 | tf_op jit(solution)/shard_map/ppermute | solution.py:24
  130.5 68.8 %all-to-all-start = ((f32[8,2,16,128]{3,2,1,0:T(8,128)}), f32[8,2,16,128]{3,2,1,0:T(8,128)}, u32[]{:S(2)}, u32[]{:S(2)}) async-start(f32[8,2,16,128]{3,2,1,0:T(8,128)} %copy.297), calls=%async_computation | async-start | bytes 262144 | tf_op jit(solution)/shard_map/all_to_all | solution.py:162
  154.5 19.3 %copy-start.4 = (f32[24,128,128]{2,1,0:T(8,128)S(1)}, f32[24,128,128]{2,1,0:T(8,128)}, u32[]{:S(2)}) copy-start(f32[24,128,128]{2,1,0:T(8,128)} %param.14) | copy-start | bytes 4718596
  154.5 19.3 %copy-start.5 = (f32[3,1,128,128]{3,2,1,0:T(8,128)S(1)}, f32[3,1,128,128]{3,2,1,0:T(8,128)}, u32[]{:S(2)}) copy-start(f32[3,1,128,128]{3,2,1,0:T(8,128)} %get-tuple-element.69) | copy-start | bytes 589828
  154.5 19.3 %copy-start.6 = (f32[3,1,128,128]{3,2,1,0:T(8,128)S(1)}, f32[3,1,128,128]{3,2,1,0:T(8,128)}, u32[]{:S(2)}) copy-start(f32[3,1,128,128]{3,2,1,0:T(8,128)} %get-tuple-element.73) | copy-start | bytes 589828
  154.5 19.3 %copy-start.7 = (f32[3,1,128,128]{3,2,1,0:T(8,128)S(1)}, f32[3,1,128,128]{3,2,1,0:T(8,128)}, u32[]{:S(2)}) copy-start(f32[3,1,128,128]{3,2,1,0:T(8,128)} %get-tuple-element.77) | copy-start | bytes 589828
  154.5 19.3 %copy-start.8 = (f32[3,1,128,128]{3,2,1,0:T(8,128)S(1)}, f32[3,1,128,128]{3,2,1,0:T(8,128)}, u32[]{:S(2)}) copy-start(f32[3,1,128,128]{3,2,1,0:T(8,128)} %get-tuple-element.81) | copy-start | bytes 589828
  154.5 19.3 %copy-start.9 = (f32[3,1,128,128]{3,2,1,0:T(8,128)S(1)}, f32[3,1,128,128]{3,2,1,0:T(8,128)}, u32[]{:S(2)}) copy-start(f32[3,1,128,128]{3,2,1,0:T(8,128)} %get-tuple-element.85) | copy-start | bytes 589828
  154.5 19.3 %copy-start.10 = (f32[3,1,128,128]{3,2,1,0:T(8,128)S(1)}, f32[3,1,128,128]{3,2,1,0:T(8,128)}, u32[]{:S(2)}) copy-start(f32[3,1,128,128]{3,2,1,0:T(8,128)} %get-tuple-element.89) | copy-start | bytes 589828
  154.5 19.3 %copy-start.11 = (f32[3,1,128,128]{3,2,1,0:T(8,128)S(1)}, f32[3,1,128,128]{3,2,1,0:T(8,128)}, u32[]{:S(2)}) copy-start(f32[3,1,128,128]{3,2,1,0:T(8,128)} %get-tuple-element.93) | copy-start | bytes 589828
  154.5 19.3 %copy-start.12 = (f32[3,1,128,128]{3,2,1,0:T(8,128)S(1)}, f32[3,1,128,128]{3,2,1,0:T(8,128)}, u32[]{:S(2)}) copy-start(f32[3,1,128,128]{3,2,1,0:T(8,128)} %get-tuple-element.97) | copy-start | bytes 589828
  154.6 19.3 %copy-start.13 = (f32[3,1,128,128]{3,2,1,0:T(8,128)S(1)}, f32[3,1,128,128]{3,2,1,0:T(8,128)}, u32[]{:S(2)}) copy-start(f32[3,1,128,128]{3,2,1,0:T(8,128)} %get-tuple-element.64) | copy-start | bytes 589828
  154.6 19.3 %copy-start.14 = (f32[3,1,128,128]{3,2,1,0:T(8,128)S(1)}, f32[3,1,128,128]{3,2,1,0:T(8,128)}, u32[]{:S(2)}) copy-start(f32[3,1,128,128]{3,2,1,0:T(8,128)} %get-tuple-element.67) | copy-start | bytes 589828
  154.6 19.3 %copy-start.15 = (f32[3,1,128,128]{3,2,1,0:T(8,128)S(1)}, f32[3,1,128,128]{3,2,1,0:T(8,128)}, u32[]{:S(2)}) copy-start(f32[3,1,128,128]{3,2,1,0:T(8,128)} %get-tuple-element.71) | copy-start | bytes 589828
  154.6 19.3 %copy-start.16 = (f32[3,1,128,128]{3,2,1,0:T(8,128)S(1)}, f32[3,1,128,128]{3,2,1,0:T(8,128)}, u32[]{:S(2)}) copy-start(f32[3,1,128,128]{3,2,1,0:T(8,128)} %get-tuple-element.75) | copy-start | bytes 589828
  154.6 19.3 %copy-start.17 = (f32[3,1,128,128]{3,2,1,0:T(8,128)S(1)}, f32[3,1,128,128]{3,2,1,0:T(8,128)}, u32[]{:S(2)}) copy-start(f32[3,1,128,128]{3,2,1,0:T(8,128)} %get-tuple-element.79) | copy-start | bytes 589828
  154.6 19.3 %copy-start.18 = (f32[3,1,128,128]{3,2,1,0:T(8,128)S(1)}, f32[3,1,128,128]{3,2,1,0:T(8,128)}, u32[]{:S(2)}) copy-start(f32[3,1,128,128]{3,2,1,0:T(8,128)} %get-tuple-element.83) | copy-start | bytes 589828
  154.6 19.3 %copy-start.19 = (f32[3,1,128,128]{3,2,1,0:T(8,128)S(1)}, f32[3,1,128,128]{3,2,1,0:T(8,128)}, u32[]{:S(2)}) copy-start(f32[3,1,128,128]{3,2,1,0:T(8,128)} %get-tuple-element.87) | copy-start | bytes 589828
  154.6 19.3 %copy-start.20 = (f32[3,1,128,128]{3,2,1,0:T(8,128)S(1)}, f32[3,1,128,128]{3,2,1,0:T(8,128)}, u32[]{:S(2)}) copy-start(f32[3,1,128,128]{3,2,1,0:T(8,128)} %get-tuple-element.91) | copy-start | bytes 589828
  191.1 54.4 %copy-start.38 = (f32[8,6]{1,0:T(8,128)S(1)}, f32[8,6]{1,0:T(8,128)}, u32[]{:S(2)}) copy-start(f32[8,6]{1,0:T(8,128)} %copy-done.37) | copy-start | bytes 580
  246.7 91.5 %copy-start.45 = (s32[8]{0:T(128)S(1)}, s32[8]{0:T(128)}, u32[]{:S(2)}) copy-start(s32[8]{0:T(128)} %bitcast_select_fusion.1) | copy-start | bytes 100
  247.1 95.6 %copy-start.24 = (f32[128,128]{1,0:T(8,128)S(1)}, f32[128,128]{1,0:T(8,128)}, u32[]{:S(2)}) copy-start(f32[128,128]{1,0:T(8,128)} %get-tuple-element.139) | copy-start | bytes 196612
  329.1 9.1 %all-to-all-start.1 = ((f32[8,1,16,128]{3,2,1,0:T(8,128)}), f32[8,1,16,128]{3,2,1,0:T(8,128)S(1)}, u32[]{:S(2)}, u32[]{:S(2)}) async-start(f32[8,1,16,128]{3,2,1,0:T(8,128)} %copy.324), calls=%async_computation.1 | async-start | bytes 131072 | tf_op jit(solution)/shard_map/all_to_all | solution.py:211
  338.4 6.9 %collective-permute-start.4 = (f32[1,128]{1,0:T(1,128)S(1)}, f32[1,128]{1,0:T(1,128)S(1)}, u32[]{:S(2)}, u32[]{:S(2)}) collective-permute-start(f32[1,128]{1,0:T(1,128)S(1)} %get-tuple-element.174), channel_id=1, source_target_pairs={{0,4},{4,8},{8,12},{12,16},{16,20},{20,24},{24,28},{28,0},{1,5},{5... | collective-permute-start | bytes 1544 | tf_op jit(solution)/shard_map/ppermute | solution.py:24
  338.6 6.8 %collective-permute-start.5 = (f32[1,128]{1,0:T(1,128)S(1)}, f32[1,128]{1,0:T(1,128)S(1)}, u32[]{:S(2)}, u32[]{:S(2)}) collective-permute-start(f32[1,128]{1,0:T(1,128)S(1)} %get-tuple-element.175), channel_id=1, source_target_pairs={{4,0},{8,4},{12,8},{16,12},{20,16},{24,20},{28,24},{0,28},{5,1},{9... | collective-permute-start | bytes 1544 | tf_op jit(solution)/shard_map/ppermute | solution.py:27
  345.5 3.9 %collective-permute-start.6 = (f32[130,1]{1,0:T(8,128)S(1)}, f32[130,1]{1,0:T(8,128)S(1)}, u32[]{:S(2)}, u32[]{:S(2)}) collective-permute-start(f32[130,1]{1,0:T(8,128)S(1)} %get-tuple-element.172), channel_id=1, source_target_pairs={{0,1},{1,2},{2,3},{3,0},{4,5},{5,6},{6,7},{7,4},{8,9},{9,10},{10,1... | collective-permute-start | bytes 1568 | tf_op jit(solution)/shard_map/ppermute | solution.py:24
  347.4 3.8 %collective-permute-start.7 = (f32[130,1]{1,0:T(8,128)S(1)}, f32[130,1]{1,0:T(8,128)S(1)}, u32[]{:S(2)}, u32[]{:S(2)}) collective-permute-start(f32[130,1]{1,0:T(8,128)S(1)} %get-tuple-element.173), channel_id=1, source_target_pairs={{1,0},{2,1},{3,2},{0,3},{5,4},{6,5},{7,6},{4,7},{9,8},{10,9},{11,1... | collective-permute-start | bytes 1568 | tf_op jit(solution)/shard_map/ppermute | solution.py:27
  (28 other events, 389.1 us)
where the time goes:
time: 355 us; the launch traced here: 353 us
  blocking collectives  164 us (46%)
  other arithmetic  100 us (28%)
  local copies, waits for them, and re-layouts  57.2 us (16%)
  starting transfers between devices  20.6 us (6%)
  waiting for transfers between devices  6.84 us (2%)
    all_gather x4, blocking collectives, operator(): lax.all_gather(edges[None], ('bx', 'by'), axis=0, tiled=True)  164 us
    add x1, other arithmetic, shards(): mixed = fields + MIX_RATE * horizontal_mix(fields_rim, ocean_rim)  19.7 us
    div x1, other arithmetic, vertical_solve(): value = (rhs[:, level] + lower * values[-1]) / denom  19 us
    div x1, other arithmetic, vertical_solve(): ratios.append(-upper / denom)  18.5 us
    unnamed x16, other arithmetic  17.8 us
    unnamed x117, local copies, waits for them, and re-layouts  12.7 us
    slice x4, local copies, waits for them, and re-layouts, padded_2(): lax.slice_in_dim(block, block.shape[dim] - width, None, axis=dim)  10.9 us
    ppermute x4, starting transfers between devices, padded_2(): lax.ppermute(lax.slice_in_dim(block, 0, width, axis=dim), axis, backward)  9.44 us
  transfers between devices with their start and end apart: 10, of which 2 were waited for; matrix products, arithmetic and copies ran while one was open for 31% of the time, Pallas kernels for 0%

commit v1 on v0

v1 whole, which is shorter than its diff:
```python
import functools

import jax
import jax.numpy as jnp
from jax import lax
from jax.experimental import pallas as pl
from jax.experimental.pallas import tpu as pltpu
from jax.sharding import PartitionSpec as P

ITERS = 4
MIX_RATE = 0.2
DIV_SCALE = 0.1
GRAVITY_STEP = 0.5
LOW_BOUND = 0.04
HIGH_BOUND = 2.0

RIM = 8
CHUNK = 32
MESH = pl.DeviceIdType.MESH


def shift(value, step, axis):
    return pltpu.roll(value, (-step) % value.shape[axis], axis)


def kernel(
    counts,
    tracer,
    velocity,
    vert_diff,
    vert_visc,
    flux,
    wind,
    surface_coef,
    height,
    land,
    table,
    tracer_out,
    velocity_out,
    height_out,
    fields,
    diff,
    visc,
    solved_t,
    solved_v,
    ocean,
    weights,
    trans,
    packed,
    halo_p,
    row_send,
    row_recv,
    col_send,
    col_recv,
    start,
    halo_s,
    blocks_send,
    blocks_recv,
    fresh_send,
    fresh_recv,
    surface,
    grad,
    ratio,
    value,
    load_sem,
    out_sem,
    send_sem,
    recv_sem,
):
    n_x, n_y = counts
    levels, width_x, width_y = diff.shape
    slots, block_len = height.shape[1], height.shape[2]
    blocks = width_x // block_len
    total_blocks = land.shape[0]
    full_x = width_x + 2 * RIM
    top = RIM + width_x
    d = lax.axis_index("bx")
    r = lax.axis_index("by")
    east, west = lax.rem(d + 1, n_x), lax.rem(d + n_x - 1, n_x)
    north, south = lax.rem(r + 1, n_y), lax.rem(r + n_y - 1, n_y)
    thickness = [1.0 + k / levels for k in range(levels)]

    loads = []

    def load(src, dst):
        copy = pltpu.make_async_copy(src, dst, load_sem.at[len(loads)])
        copy.start()
        loads.append(copy)
        return copy

    rows = pl.ds(RIM, width_x)
    load_v = [
        load(velocity.at[c], fields.at[pl.ds((1 + c) * levels, levels), rows, :]) for c in range(2)
    ]
    load_t = load(tracer, fields.at[pl.ds(0, levels), rows, :])
    load_diff = load(vert_diff, diff)
    load_visc = load(vert_visc, visc)

    barrier = pltpu.get_barrier_semaphore()
    peers = [(lax.rem(d + step, n_x), r) for step in range(1, n_x)]
    peers += [(x, y) for y in (north, south) for x in (west, d, east)]
    for peer in peers:
        pl.semaphore_signal(barrier, inc=1, device_id=peer, device_id_type=MESH)

    sends = []

    def send(src, dst, peer):
        at = len(sends)
        copy = pltpu.make_async_remote_copy(
            src_ref=src,
            dst_ref=dst,
            send_sem=send_sem.at[at],
            recv_sem=recv_sem.at[at],
            device_id=peer,
            device_id_type=MESH,
        )
        copy.start()
        sends.append(copy)
        return copy

    slot_for = []
    for t in range(n_x):
        found = jnp.int32(-1)
        for j in range(blocks):
            off = table[t * blocks + j, r] - d * slots
            found = jnp.where((off >= 0) & (off < slots), off, found)
        slot_for.append(found)
        block = height[0, jnp.maximum(found, 0)]
        blocks_send[t] = jnp.where(found >= 0, block, 0.0)
    own_pos = [table[d * blocks + j, r] for j in range(blocks)]
    holder = [lax.div(jnp.maximum(pos, 0), jnp.int32(slots)) for pos in own_pos]

    lane = lax.broadcasted_iota(jnp.int32, (block_len, width_y), 1)
    row_north, row_south = jnp.minimum(r + 1, n_y - 1), jnp.maximum(r - 1, 0)
    for b in range(-1, blocks + 1):
        block_id = lax.rem(d * blocks + b + total_blocks, total_blocks)
        here = 1 - land[block_id, r]
        up = jnp.where(r < n_y - 1, 1 - land[block_id, row_north], 0)
        down = jnp.where(r > 0, 1 - land[block_id, row_south], 0)
        size = block_len if 0 <= b < blocks else RIM
        first = 0 if b < 0 else RIM + b * block_len
        at = pl.ds(first, size)
        ocean[at, :width_y] = jnp.full((size, width_y), here).astype(jnp.float32)
        ocean[at, width_y:] = jnp.where(lane[:size] < width_y // 2, up, down).astype(jnp.float32)

    pl.semaphore_wait(barrier, len(peers))
    a2a = [
        send(blocks_send.at[peers[i][0]], blocks_recv.at[d], peers[i]) for i in range(n_x - 1)
    ]
    blocks_recv[d] = blocks_send[d]

    for copy in load_v:
        copy.wait()
    for c in range(2):

        def add(k, total, c=c):
            scale = 1.0 + k.astype(jnp.float32) / levels
            return total + scale * fields[(1 + c) * levels + k, pl.ds(RIM, width_x), :]

        trans[c, pl.ds(RIM, width_x), :width_y] = lax.fori_loop(
            0, levels, add, jnp.zeros((width_x, width_y), jnp.float32), unroll=4
        )
    trans[2, pl.ds(RIM, width_x), :width_y] = surface_coef[...]
    wide = lax.broadcasted_iota(jnp.int32, (width_x, width_y), 1)
    half = width_y // 2
    t0 = trans[0, pl.ds(RIM, width_x), :width_y]
    t1 = trans[1, pl.ds(RIM, width_x), :width_y]
    t2 = surface_coef[...]
    low = jnp.where(
        wide < RIM, t0, jnp.where(wide < 2 * RIM, shift(t1, -RIM, 1), shift(t2, -2 * RIM, 1))
    )
    high = jnp.where(
        wide >= width_y - RIM,
        t0,
        jnp.where(wide >= width_y - 2 * RIM, shift(t1, RIM, 1), shift(t2, 2 * RIM, 1)),
    )
    packed[...] = jnp.where(wide < half, low, high)

    def halo(source_at, side_at, target, corners):
        out = []
        for to, peer_y in ((1, north), (0, south)):
            out.append(send(side_at(0, width_x), target.at[to, pl.ds(RIM, width_x), :], (d, peer_y)))
            out.append(
                send(side_at(width_x - RIM, RIM), target.at[to, pl.ds(0, RIM), :], (east, peer_y))
            )
            out.append(send(side_at(0, RIM), target.at[to, pl.ds(top, RIM), :], (west, peer_y)))
        out.append(send(source_at(width_x), corners(0), (east, d_row)))
        out.append(send(source_at(RIM), corners(top), (west, d_row)))
        return out

    d_row = r
    halo_trans = halo(
        lambda first: trans.at[:, pl.ds(first, RIM), pl.ds(0, width_y)],
        lambda first, size: packed.at[pl.ds(first, size), :],
        halo_p,
        lambda first: trans.at[:, pl.ds(first, RIM), pl.ds(0, width_y)],
    )

    load_t.wait()
    row_send[0] = fields[:, RIM, :]
    row_send[1] = fields[:, top - 1, :]
    row_copies = [
        send(row_send.at[1], row_recv.at[0], (east, r)),
        send(row_send.at[0], row_recv.at[1], (west, r)),
    ]
    lane_c = lax.broadcasted_iota(jnp.int32, (CHUNK, width_y), 1)

    def pack(i, carry):
        first = pl.multiple_of(i * CHUNK, CHUNK)
        low_cols = jnp.zeros((CHUNK, width_y), jnp.float32)
        high_cols = jnp.zeros((CHUNK, width_y), jnp.float32)
        for k in range(3 * levels):
            block = fields[k, pl.ds(first + RIM, CHUNK), :]
            low_cols = jnp.where(lane_c == k, block[:, :1], low_cols)
            high_cols = jnp.where(lane_c == k, block[:, width_y - 1 :], high_cols)
        col_send[0, pl.ds(first, CHUNK), :] = low_cols
        col_send[1, pl.ds(first, CHUNK), :] = high_cols
        return carry

    lax.fori_loop(0, width_x // CHUNK, pack, 0)
    col_copies = [
        send(col_send.at[1], col_recv.at[0], (d, north)),
        send(col_send.at[0], col_recv.at[1], (d, south)),
    ]

    for copy in a2a:
        copy.wait_recv()
    for j in range(blocks):
        at = pl.ds(RIM + j * block_len, block_len)
        start[at, :width_y] = ocean[at, :width_y] * blocks_recv[holder[j]]
    halo_start = halo(
        lambda first: start.at[pl.ds(first, RIM), pl.ds(0, width_y)],
        lambda first, size: start.at[pl.ds(RIM + first, size), pl.ds(0, width_y)],
        halo_s,
        lambda first: start.at[pl.ds(first, RIM), pl.ds(0, width_y)],
    )

    rim = ocean[...]
    inner = lambda padded: padded[RIM:top, :width_y]
    centre = inner(rim)
    total = jnp.zeros_like(centre)
    for at, (step, axis) in enumerate(((1, 0), (-1, 0), (1, 1), (-1, 1))):
        weight = MIX_RATE * (centre * inner(shift(rim, step, axis)))
        weights[1 + at] = weight
        total = total + weight
    weights[0] = 1.0 - total

    for copy in row_copies + col_copies:
        copy.wait_recv()
    fields[:, RIM - 1, :] = row_recv[0]
    fields[:, top, :] = row_recv[1]

    def columns(first_field, count, coef_ref, forcing, out_ref, final):
        def body(i, carry):
            first = pl.multiple_of(i * CHUNK, CHUNK)
            at = pl.ds(first, CHUNK)
            w0, w_e, w_w, w_n, w_s = [weights[n, at, :] for n in range(5)]
            below = col_recv[0, at, :]
            above = col_recv[1, at, :]
            gain = None
            last = [None] * count
            coef_up = None
            for k in range(levels):
                inv_thick = 1.0 / thickness[k]
                if k < levels - 1:
                    coef = coef_ref[k, at, :]
                    upper = coef * inv_thick
                if k > 0:
                    lower = coef_up * inv_thick
                if k == 0:
                    denom = 1.0 + upper
                elif k < levels - 1:
                    denom = (1.0 + upper) + lower * (1.0 - gain)
                else:
                    denom = 1.0 + lower * (1.0 - gain)
                inverse = 1.0 / denom
                if k < levels - 1:
                    gain = upper * inverse
                    ratio[k] = gain
                    coef_up = coef
                for f in range(count):
                    n = (first_field + f) * levels + k
                    block = fields[n, pl.ds(first, CHUNK + 2 * RIM), :]
                    mid = block[RIM : RIM + CHUNK]
                    near_n = jnp.where(
                        lane_c == width_y - 1, above[:, n : n + 1], shift(mid, 1, 1)
                    )
                    near_s = jnp.where(lane_c == 0, below[:, n : n + 1], shift(mid, -1, 1))
                    rhs = (
                        w0 * mid
                        + w_e * block[RIM + 1 : RIM + 1 + CHUNK]
                        + w_w * block[RIM - 1 : RIM - 1 + CHUNK]
                        + (w_n * near_n + w_s * near_s)
                    )
                    if k == 0:
                        rhs = rhs + forcing(f, at) / thickness[0]
                    else:
                        rhs = rhs + lower * last[f]
                    last[f] = rhs * inverse
                    if k < levels - 1:
                        value[f, k] = last[f]
            mask = ocean[pl.ds(first + RIM, CHUNK), :width_y]
            for k in range(levels - 1, -1, -1):
                for f in range(count):
                    if k < levels - 1:
                        last[f] = value[f, k] + ratio[k] * last[f]
                    out_ref[f * levels + k, at, :] = final(f, mask * last[f], at)
            return carry

        lax.fori_loop(0, width_x // CHUNK, body, 0)

    load_diff.wait()
    columns(0, 1, diff, lambda f, at: flux[at, :], solved_t, lambda f, x, at: x)
    out_t = pltpu.make_async_copy(solved_t, tracer_out, out_sem.at[0])
    out_t.start()

    for copy in halo_trans + halo_start:
        copy.wait_recv()
    full = lax.broadcasted_iota(jnp.int32, (full_x, width_y), 1)
    from_n, from_s = halo_p[0], halo_p[1]
    trans[0, :, width_y:] = jnp.where(full < half, from_n, from_s)
    trans[1, :, width_y:] = jnp.where(full < half, shift(from_n, RIM, 1), shift(from_s, -RIM, 1))
    trans[2, :, width_y:] = jnp.where(
        full < RIM,
        shift(from_n, 2 * RIM, 1),
        jnp.where(full >= width_y - RIM, shift(from_s, -2 * RIM, 1), 1.0),
    )
    start[:, width_y:] = ocean[:, width_y:] * jnp.where(full < half, halo_s[0], halo_s[1])
    wet = ocean[...]
    t0 = wet * trans[0]
    t1 = wet * trans[1]
    coef = trans[2]
    divergence = wet * (
        0.5 * ((shift(t0, 1, 0) - shift(t0, -1, 0)) + (shift(t1, 1, 1) - shift(t1, -1, 1)))
    )
    result = wet * start[...]
    source = wet * coef * result - DIV_SCALE * divergence
    diagonal = coef + 6.0
    inverse = 1.0 / diagonal

    def residual_of(field):
        pair = shift(field, 1, 0) + shift(field, -1, 0)
        mixed = field + 0.5 * pair
        near = pair + (shift(mixed, 1, 1) + shift(mixed, -1, 1))
        return source - wet * (diagonal * field - near)

    scale_a = 2.0 / (HIGH_BOUND - LOW_BOUND)
    gamma = (HIGH_BOUND + LOW_BOUND) / 2.0
    update = residual_of(result) * inverse * (1.0 / gamma)
    result = result + update
    weight = 2.0 / gamma
    for step in range(1, ITERS):
        weight = 1.0 / (gamma - weight / (4.0 * scale_a * scale_a))
        update = weight * (residual_of(result) * inverse) + (gamma * weight - 1.0) * update
        result = result + update
    for j in range(blocks):
        first = RIM + j * block_len
        surface[j] = result[first : first + block_len, :width_y]
    for t in range(n_x):
        found = jnp.int32(-1)
        for j in range(blocks):
            found = jnp.where((holder[j] == t) & (own_pos[j] >= 0), jnp.int32(j), found)
        fresh_send[t] = surface[jnp.maximum(found, 0)]
    fresh = [send(fresh_send.at[peers[i][0]], fresh_recv.at[d], peers[i]) for i in range(n_x - 1)]
    fresh_recv[d] = fresh_send[d]
    step_scale = GRAVITY_STEP * 0.5
    grad[0] = inner(wet * (step_scale * (shift(result, 1, 0) - shift(result, -1, 0))))
    grad[1] = inner(wet * (step_scale * (shift(result, 1, 1) - shift(result, -1, 1))))

    load_visc.wait()
    columns(
        1, 2, visc, lambda f, at: wind[f, at, :], solved_v, lambda f, x, at: x - grad[f, at, :]
    )
    out_v = [
        pltpu.make_async_copy(
            solved_v.at[pl.ds(c * levels, levels)], velocity_out.at[c], out_sem.at[1 + c]
        )
        for c in range(2)
    ]
    for copy in out_v:
        copy.start()

    for copy in fresh:
        copy.wait_recv()
    for s in range(slots):
        source_at = jnp.int32(0)
        for t in range(n_x):
            source_at = jnp.where(slot_for[t] == s, jnp.int32(t), source_at)
        height_out[0, s] = fresh_recv[source_at]
    for copy in sends:
        copy.wait_send()
    for copy in [out_t] + out_v:
        copy.wait()


def shards(counts, *args):
    tracer, velocity, height = args[0], args[1], args[7]
    levels, width_x, width_y = tracer.shape
    slots, block_len = height.shape[1], height.shape[2]
    blocks = width_x // block_len
    n_x, n_y = counts
    full_x = width_x + 2 * RIM
    n_sends = 2 * (n_x - 1) + 2 * 8 + 4
    f32 = jnp.float32
    vmem = pl.BlockSpec(memory_space=pltpu.VMEM)
    smem = pl.BlockSpec(memory_space=pltpu.SMEM)
    hbm = pl.BlockSpec(memory_space=pl.ANY)
    scratch = [
        pltpu.VMEM((3 * levels, full_x, width_y), f32),
        pltpu.VMEM((levels, width_x, width_y), f32),
        pltpu.VMEM((levels, width_x, width_y), f32),
        pltpu.VMEM((levels, width_x, width_y), f32),
        pltpu.VMEM((2 * levels, width_x, width_y), f32),
        pltpu.VMEM((full_x, 2 * width_y), f32),
        pltpu.VMEM((5, width_x, width_y), f32),
        pltpu.VMEM((3, full_x, 2 * width_y), f32),
        pltpu.VMEM((width_x, width_y), f32),
        pltpu.VMEM((2, full_x, width_y), f32),
        pltpu.VMEM((2, 3 * levels, width_y), f32),
        pltpu.VMEM((2, 3 * levels, width_y), f32),
        pltpu.VMEM((2, width_x, width_y), f32),
        pltpu.VMEM((2, width_x, width_y), f32),
        pltpu.VMEM((full_x, 2 * width_y), f32),
        pltpu.VMEM((2, full_x, width_y), f32),
        pltpu.VMEM((n_x, block_len, width_y), f32),
        pltpu.VMEM((n_x, block_len, width_y), f32),
        pltpu.VMEM((n_x, block_len, width_y), f32),
        pltpu.VMEM((n_x, block_len, width_y), f32),
        pltpu.VMEM((blocks, block_len, width_y), f32),
        pltpu.VMEM((2, width_x, width_y), f32),
        pltpu.VMEM((levels, CHUNK, width_y), f32),
        pltpu.VMEM((2, levels, CHUNK, width_y), f32),
        pltpu.SemaphoreType.DMA((5,)),
        pltpu.SemaphoreType.DMA((3,)),
        pltpu.SemaphoreType.DMA((n_sends,)),
        pltpu.SemaphoreType.DMA((n_sends,)),
    ]
    return pl.pallas_call(
        functools.partial(kernel, counts),
        out_shape=(
            jax.ShapeDtypeStruct(tracer.shape, f32),
            jax.ShapeDtypeStruct(velocity.shape, f32),
            jax.ShapeDtypeStruct(height.shape, f32),
        ),
        in_specs=[hbm, hbm, hbm, hbm, vmem, vmem, vmem, vmem, smem, smem],
        out_specs=(hbm, hbm, vmem),
        scratch_shapes=scratch,
        compiler_params=pltpu.CompilerParams(
            collective_id=0, has_side_effects=True, vmem_limit_bytes=40 * 1024 * 1024
        ),
        cost_estimate=pl.CostEstimate(
            flops=40 * 3 * levels * width_x * width_y,
            bytes_accessed=8 * 4 * levels * width_x * width_y,
            transcendentals=0,
        ),
    )(*args)


def solution(mesh):
    placed = (
        P(None, "bx", "by"),
        P(None, None, "bx", "by"),
        P(None, "bx", "by"),
        P(None, "bx", "by"),
        P("bx", "by"),
        P(None, "bx", "by"),
        P("bx", "by"),
        P("by", "bx", None, None),
        P(),
        P(),
    )
    return jax.shard_map(
        functools.partial(shards, (mesh.shape["bx"], mesh.shape["by"])),
        mesh=mesh,
        in_specs=placed,
        out_specs=(P(None, "bx", "by"), P(None, None, "bx", "by"), P("by", "bx", None, None)),
        check_vma=False,
    )
```

time: 355 us -> 41.5 us (0.12)
  blocking collectives: 164 us -> 0 us
  other arithmetic: 100 us -> 0 us
  local copies, waits for them, and re-layouts: 57.2 us -> 14.5 us
  Pallas kernels: 0 us -> 25.9 us
  starting transfers between devices: 20.6 us -> 0 us
  waiting for transfers between devices: 6.84 us -> 0 us
    all_gather x4 -> x0, blocking collectives: 164 us -> none  [operator(): lax.all_gather(edges[None], ('bx', 'by'), axis=0, tiled=True)]
    div x2 -> x0, other arithmetic: 37.6 us -> none  [the longest x1 19 us: vertical_solve(): value = (rhs[:, level] + lower * values[-1]) / denom]
    pallas_call x0 -> x1, Pallas kernels: none -> 25.9 us  [shards(): pl.pallas_call(functools.partial(kernel, counts), out_shape=(jax.ShapeDty...]
    add x8 -> x0, other arithmetic: 20.6 us -> none  [the longest x1 19.7 us: shards(): mixed = fields + MIX_RATE * horizontal_mix(fields_rim, ocean_rim)]
    slice x45 -> x0, local copies, waits for them, and re-layouts: 20.3 us -> none  [the longest x4 10.9 us: padded_2(): lax.slice_in_dim(block, block.shape[dim] - width, None, axis=dim)]
    unnamed x16 -> x0, other arithmetic: 17.8 us -> none
    mul x11 -> x0, other arithmetic: 15 us -> none  [the longest x1 8.9 us: shards(): fields_rim = padded_2(fields, (('bx', 2), ('by', 3)), 1) * ocean_rim]
    ppermute x8 -> x0, starting transfers between devices: 13.1 us -> none  [the longest x4 9.44 us: padded_2(): lax.ppermute(lax.slice_in_dim(block, 0, width, axis=dim), axis, backward)]
  transfers between devices with their start and end apart: 10 -> 0, of which waited for: 2 -> 0; matrix products, arithmetic and copies ran while one was open for 31% -> 0% of each run, Pallas kernels for 0% -> 0%
where the time goes in v1:
time: 41.5 us; the launch traced here: 41 us
  Pallas kernels  25.9 us (62%)
  local copies, waits for them, and re-layouts  14.5 us (35%)
  between operations  0.65 us (2%)
    pallas_call x1, Pallas kernels, shards(): pl.pallas_call(functools.partial(kernel, counts), out_shape=(jax.ShapeDty...  25.9 us
    unnamed x21, local copies, waits for them, and re-layouts  14.5 us

profile of v1, /device:TPU:1, one launch (start us, length us, event | category | flops | bytes accessed | tf_op | source)
XLA Modules:
  0.0 41.0 jit_solution(12137909444892108279)
XLA Ops:
  0.6 0.8 %copy.13.land = s32[64,4]{1,0:T(8,128)S(1)} copy(s32[64,4]{0,1:T(4,128)} %param.18) | data formatting | bytes 2048 | tf_op args[8]
  1.4 0.8 %copy.14.table = s32[64,4]{1,0:T(8,128)S(1)} copy(s32[64,4]{0,1:T(4,128)} %param.19) | data formatting | bytes 2048 | tf_op args[9]
  2.2 0.0 copy-start
  2.2 1.9 %copy-done = f32[2,24,128,128]{3,2,1,0:T(8,128)S(1)} copy-done((f32[2,24,128,128]{3,2,1,0:T(8,128)S(1)}, f32[2,24,128,128]{3,2,1,0:T(8,128)}, u32[]{:S(2)}) %copy-start) | copy-done | bytes 3145752
  4.1 0.0 copy-start.1
  4.1 1.4 %copy-done.1 = f32[24,128,128]{2,1,0:T(8,128)S(1)} copy-done((f32[24,128,128]{2,1,0:T(8,128)S(1)}, f32[24,128,128]{2,1,0:T(8,128)}, u32[]{:S(2)}) %copy-start.1) | copy-done | bytes 1572888
  5.5 0.0 copy-start.2
  5.5 1.4 %copy-done.2 = f32[24,128,128]{2,1,0:T(8,128)S(1)} copy-done((f32[24,128,128]{2,1,0:T(8,128)S(1)}, f32[24,128,128]{2,1,0:T(8,128)}, u32[]{:S(2)}) %copy-start.2) | copy-done | bytes 1572888
  6.9 0.0 copy-start.3
  6.9 1.4 %copy-done.3 = f32[24,128,128]{2,1,0:T(8,128)S(1)} copy-done((f32[24,128,128]{2,1,0:T(8,128)S(1)}, f32[24,128,128]{2,1,0:T(8,128)}, u32[]{:S(2)}) %copy-start.3) | copy-done | bytes 1572888
  8.3 0.0 copy-start.4
  8.3 0.9 %copy-done.4 = f32[2,128,128]{2,1,0:T(8,128)S(1)} copy-done((f32[2,128,128]{2,1,0:T(8,128)S(1)}, f32[2,128,128]{2,1,0:T(8,128)}, u32[]{:S(2)}) %copy-start.4) | copy-done | bytes 131096
  9.2 0.0 copy-start.5
  9.2 0.8 %copy-done.5 = f32[128,128]{1,0:T(8,128)S(1)} copy-done((f32[128,128]{1,0:T(8,128)S(1)}, f32[128,128]{1,0:T(8,128)}, u32[]{:S(2)}) %copy-start.5) | copy-done | bytes 65560
  10.0 0.0 copy-start.6
  10.0 0.8 %copy-done.6 = f32[128,128]{1,0:T(8,128)S(1)} copy-done((f32[128,128]{1,0:T(8,128)S(1)}, f32[128,128]{1,0:T(8,128)}, u32[]{:S(2)}) %copy-start.6) | copy-done | bytes 65560
  10.9 0.0 copy-start.7
  10.9 0.8 %copy-done.7 = f32[1,6,16,128]{3,2,1,0:T(8,128)S(1)} copy-done((f32[1,6,16,128]{3,2,1,0:T(8,128)S(1)}, f32[1,6,16,128]{3,2,1,0:T(8,128)}, u32[]{:S(2)}) %copy-start.7) | copy-done | bytes 49176
  11.7 25.9 %shard_map.121 = (f32[24,128,128]{2,1,0:T(8,128)S(1)}, f32[2,24,128,128]{3,2,1,0:T(8,128)S(1)}, f32[1,6,16,128]{3,2,1,0:T(8,128)S(1)}) custom-call(f32[24,128,128]{2,1,0:T(8,128)S(1)} %copy-done.1, f32[2,24,128,128]{3,2,1,0:T(8,128)S(1)} %copy-done, f32[24,128,128]{2,1,0:T(8,128)S(1)} %copy-done.2, f32[24,128,128]{2,1,0:T(8,128)S(1)} %copy-done.3, ...), custom_call_target="tpu_custom_call" | custom-call | flops 47185920 | bytes 12582912 | tf_op jit(solution)/shard_map/pallas_call | solution.py:438
  37.6 1.1 %copy.18 = f32[24,128,128]{2,1,0:T(8,128)} copy(f32[24,128,128]{2,1,0:T(8,128)S(1)} %get-tuple-element.6) | data formatting | bytes 3145728
  38.7 1.7 %copy.19 = f32[2,24,128,128]{3,2,1,0:T(8,128)} copy(f32[2,24,128,128]{3,2,1,0:T(8,128)S(1)} %get-tuple-element.7) | data formatting | bytes 6291456
  40.4 0.6 %copy.20 = f32[1,6,16,128]{3,2,1,0:T(8,128)} copy(f32[1,6,16,128]{3,2,1,0:T(8,128)S(1)} %get-tuple-element.8) | data formatting | bytes 98304
Async XLA Ops:
  2.2 1.9 %copy-start = (f32[2,24,128,128]{3,2,1,0:T(8,128)S(1)}, f32[2,24,128,128]{3,2,1,0:T(8,128)}, u32[]{:S(2)}) copy-start(f32[2,24,128,128]{3,2,1,0:T(8,128)} %velocity.1) | copy-start | bytes 9437188
  4.1 1.4 %copy-start.1 = (f32[24,128,128]{2,1,0:T(8,128)S(1)}, f32[24,128,128]{2,1,0:T(8,128)}, u32[]{:S(2)}) copy-start(f32[24,128,128]{2,1,0:T(8,128)} %tracer.1) | copy-start | bytes 4718596
  5.5 1.4 %copy-start.2 = (f32[24,128,128]{2,1,0:T(8,128)S(1)}, f32[24,128,128]{2,1,0:T(8,128)}, u32[]{:S(2)}) copy-start(f32[24,128,128]{2,1,0:T(8,128)} %vert_diff.1) | copy-start | bytes 4718596
  6.9 1.4 %copy-start.3 = (f32[24,128,128]{2,1,0:T(8,128)S(1)}, f32[24,128,128]{2,1,0:T(8,128)}, u32[]{:S(2)}) copy-start(f32[24,128,128]{2,1,0:T(8,128)} %vert_visc.1) | copy-start | bytes 4718596
  8.3 0.9 %copy-start.4 = (f32[2,128,128]{2,1,0:T(8,128)S(1)}, f32[2,128,128]{2,1,0:T(8,128)}, u32[]{:S(2)}) copy-start(f32[2,128,128]{2,1,0:T(8,128)} %wind.1) | copy-start | bytes 393220
  9.2 0.8 %copy-start.5 = (f32[128,128]{1,0:T(8,128)S(1)}, f32[128,128]{1,0:T(8,128)}, u32[]{:S(2)}) copy-start(f32[128,128]{1,0:T(8,128)} %flux.1) | copy-start | bytes 196612
  10.0 0.8 %copy-start.6 = (f32[128,128]{1,0:T(8,128)S(1)}, f32[128,128]{1,0:T(8,128)}, u32[]{:S(2)}) copy-start(f32[128,128]{1,0:T(8,128)} %surface_coef.1) | copy-start | bytes 196612
  10.9 0.8 %copy-start.7 = (f32[1,6,16,128]{3,2,1,0:T(8,128)S(1)}, f32[1,6,16,128]{3,2,1,0:T(8,128)}, u32[]{:S(2)}) copy-start(f32[1,6,16,128]{3,2,1,0:T(8,128)} %height.1) | copy-start | bytes 147460

commit v2 on v1

--- a/solution.py
+++ b/solution.py
@@ -29,10 +29,10 @@
     velocity,
     vert_diff,
     vert_visc,
-    flux,
-    wind,
-    surface_coef,
-    height,
+    flux_in,
+    wind_in,
+    surface_coef_in,
+    height_in,
     land,
     table,
     tracer_out,
@@ -43,6 +43,10 @@
     visc,
     solved_t,
     solved_v,
+    flux,
+    wind,
+    surface_coef,
+    height,
     ocean,
     weights,
     trans,
@@ -71,7 +75,7 @@
     levels, width_x, width_y = diff.shape
     slots, block_len = height.shape[1], height.shape[2]
     blocks = width_x // block_len
-    total_blocks = land.shape[0]
+    total_blocks = land.shape[1]
     full_x = width_x + 2 * RIM
     top = RIM + width_x
     d = lax.axis_index("bx")
@@ -89,12 +93,16 @@
         return copy
 
     rows = pl.ds(RIM, width_x)
+    load_height = load(height_in, height)
     load_v = [
         load(velocity.at[c], fields.at[pl.ds((1 + c) * levels, levels), rows, :]) for c in range(2)
     ]
+    load_coef = load(surface_coef_in, surface_coef)
     load_t = load(tracer, fields.at[pl.ds(0, levels), rows, :])
     load_diff = load(vert_diff, diff)
+    load_flux = load(flux_in, flux)
     load_visc = load(vert_visc, visc)
+    load_wind = load(wind_in, wind)
 
     barrier = pltpu.get_barrier_semaphore()
     peers = [(lax.rem(d + step, n_x), r) for step in range(1, n_x)]
@@ -118,25 +126,26 @@
         sends.append(copy)
         return copy
 
+    load_height.wait()
     slot_for = []
     for t in range(n_x):
         found = jnp.int32(-1)
         for j in range(blocks):
-            off = table[t * blocks + j, r] - d * slots
+            off = table[r, t * blocks + j] - d * slots
             found = jnp.where((off >= 0) & (off < slots), off, found)
         slot_for.append(found)
         block = height[0, jnp.maximum(found, 0)]
         blocks_send[t] = jnp.where(found >= 0, block, 0.0)
-    own_pos = [table[d * blocks + j, r] for j in range(blocks)]
+    own_pos = [table[r, d * blocks + j] for j in range(blocks)]
     holder = [lax.div(jnp.maximum(pos, 0), jnp.int32(slots)) for pos in own_pos]
 
     lane = lax.broadcasted_iota(jnp.int32, (block_len, width_y), 1)
     row_north, row_south = jnp.minimum(r + 1, n_y - 1), jnp.maximum(r - 1, 0)
     for b in range(-1, blocks + 1):
         block_id = lax.rem(d * blocks + b + total_blocks, total_blocks)
-        here = 1 - land[block_id, r]
-        up = jnp.where(r < n_y - 1, 1 - land[block_id, row_north], 0)
-        down = jnp.where(r > 0, 1 - land[block_id, row_south], 0)
+        here = 1 - land[r, block_id]
+        up = jnp.where(r < n_y - 1, 1 - land[row_north, block_id], 0)
+        down = jnp.where(r > 0, 1 - land[row_south, block_id], 0)
         size = block_len if 0 <= b < blocks else RIM
         first = 0 if b < 0 else RIM + b * block_len
         at = pl.ds(first, size)
@@ -160,6 +169,7 @@
         trans[c, pl.ds(RIM, width_x), :width_y] = lax.fori_loop(
             0, levels, add, jnp.zeros((width_x, width_y), jnp.float32), unroll=4
         )
+    load_coef.wait()
     trans[2, pl.ds(RIM, width_x), :width_y] = surface_coef[...]
     wide = lax.broadcasted_iota(jnp.int32, (width_x, width_y), 1)
     half = width_y // 2
@@ -211,8 +221,9 @@
         high_cols = jnp.zeros((CHUNK, width_y), jnp.float32)
         for k in range(3 * levels):
             block = fields[k, pl.ds(first + RIM, CHUNK), :]
-            low_cols = jnp.where(lane_c == k, block[:, :1], low_cols)
-            high_cols = jnp.where(lane_c == k, block[:, width_y - 1 :], high_cols)
+            turned = pltpu.roll(block, k, 1) if k else block
+            low_cols = jnp.where(lane_c == k, turned, low_cols)
+            high_cols = jnp.where(lane_c == (k - 1) % width_y, turned, high_cols)
         col_send[0, pl.ds(first, CHUNK), :] = low_cols
         col_send[1, pl.ds(first, CHUNK), :] = high_cols
         return carry
@@ -250,7 +261,7 @@
     fields[:, RIM - 1, :] = row_recv[0]
     fields[:, top, :] = row_recv[1]
 
-    def columns(first_field, count, coef_ref, forcing, out_ref, final):
+    def columns(first_field, count, coef_ref, forcing, store, after=None):
         def body(i, carry):
             first = pl.multiple_of(i * CHUNK, CHUNK)
             at = pl.ds(first, CHUNK)
@@ -285,7 +296,9 @@
                     near_n = jnp.where(
                         lane_c == width_y - 1, above[:, n : n + 1], shift(mid, 1, 1)
                     )
-                    near_s = jnp.where(lane_c == 0, below[:, n : n + 1], shift(mid, -1, 1))
+                    near_s = jnp.where(
+                        lane_c == 0, below[:, (n - 1) % width_y][:, None], shift(mid, -1, 1)
+                    )
                     rhs = (
                         w0 * mid
                         + w_e * block[RIM + 1 : RIM + 1 + CHUNK]
@@ -304,14 +317,25 @@
                 for f in range(count):
                     if k < levels - 1:
                         last[f] = value[f, k] + ratio[k] * last[f]
-                    out_ref[f * levels + k, at, :] = final(f, mask * last[f], at)
+                    store(f, k, at, mask * last[f])
             return carry
 
-        lax.fori_loop(0, width_x // CHUNK, body, 0)
+        def step(i, carry):
+            body(i, carry)
+            if after is not None:
+                after(i).start()
+            return carry
+
+        lax.fori_loop(0, width_x // CHUNK, step, 0)
 
     load_diff.wait()
-    columns(0, 1, diff, lambda f, at: flux[at, :], solved_t, lambda f, x, at: x)
-    out_t = pltpu.make_async_copy(solved_t, tracer_out, out_sem.at[0])
+    load_flux.wait()
+
+    def store_t(f, k, at, x):
+        solved_t[k, at, :] = x
+
+    columns(0, 1, diff, lambda f, at: flux[at, :], store_t)
+    out_t = pltpu.make_async_copy(solved_t, tracer_out, out_sem.at[width_x // CHUNK])
     out_t.start()
 
     for copy in halo_trans + halo_start:
@@ -368,17 +392,18 @@
     grad[1] = inner(wet * (step_scale * (shift(result, 1, 1) - shift(result, -1, 1))))
 
     load_visc.wait()
-    columns(
-        1, 2, visc, lambda f, at: wind[f, at, :], solved_v, lambda f, x, at: x - grad[f, at, :]
-    )
-    out_v = [
-        pltpu.make_async_copy(
-            solved_v.at[pl.ds(c * levels, levels)], velocity_out.at[c], out_sem.at[1 + c]
+    load_wind.wait()
+
+    def store_v(f, k, at, x):
+        solved_v[f, k, at, :] = x - grad[f, at, :]
+
+    def out_v(i):
+        at = pl.ds(pl.multiple_of(i * CHUNK, CHUNK), CHUNK)
+        return pltpu.make_async_copy(
+            solved_v.at[:, :, at, :], velocity_out.at[:, :, at, :], out_sem.at[i]
         )
-        for c in range(2)
-    ]
-    for copy in out_v:
-        copy.start()
+
+    columns(1, 2, visc, lambda f, at: wind[f, at, :], store_v, out_v)
 
     for copy in fresh:
         copy.wait_recv()
@@ -389,7 +414,26 @@
         height_out[0, s] = fresh_recv[source_at]
     for copy in sends:
         copy.wait_send()
-    for copy in [out_t] + out_v:
+    out_t.wait()
+    for i in range(width_x // CHUNK):
+        out_v(i).wait()
+
+
+def write_out(a, b, c, a_out, b_out, c_out, a_held, b_held, c_held, in_sems, out_sems):
+    pieces = [(c, c_held, c_out)]
+    third = a.shape[0] // 3
+    for i in range(3):
+        at = pl.ds(i * third, third)
+        pieces.append((a.at[at], a_held.at[at], a_out.at[at]))
+        pieces += [(b.at[n, at], b_held.at[n, at], b_out.at[n, at]) for n in range(2)]
+    reads = [pltpu.make_async_copy(x, h, in_sems.at[i]) for i, (x, h, _) in enumerate(pieces)]
+    writes = [pltpu.make_async_copy(h, y, out_sems.at[i]) for i, (_, h, y) in enumerate(pieces)]
+    for copy in reads:
+        copy.start()
+    for read, write in zip(reads, writes):
+        read.wait()
+        write.start()
+    for copy in writes:
         copy.wait()
 
 
@@ -404,13 +448,17 @@
     f32 = jnp.float32
     vmem = pl.BlockSpec(memory_space=pltpu.VMEM)
     smem = pl.BlockSpec(memory_space=pltpu.SMEM)
-    hbm = pl.BlockSpec(memory_space=pl.ANY)
+    hbm = pl.BlockSpec(memory_space=pltpu.HBM)
     scratch = [
         pltpu.VMEM((3 * levels, full_x, width_y), f32),
         pltpu.VMEM((levels, width_x, width_y), f32),
         pltpu.VMEM((levels, width_x, width_y), f32),
         pltpu.VMEM((levels, width_x, width_y), f32),
-        pltpu.VMEM((2 * levels, width_x, width_y), f32),
+        pltpu.VMEM((2, levels, width_x, width_y), f32),
+        pltpu.VMEM((width_x, width_y), f32),
+        pltpu.VMEM((2, width_x, width_y), f32),
+        pltpu.VMEM((width_x, width_y), f32),
+        pltpu.VMEM(height.shape, f32),
         pltpu.VMEM((full_x, 2 * width_y), f32),
         pltpu.VMEM((5, width_x, width_y), f32),
         pltpu.VMEM((3, full_x, 2 * width_y), f32),
@@ -430,30 +478,39 @@
         pltpu.VMEM((2, width_x, width_y), f32),
         pltpu.VMEM((levels, CHUNK, width_y), f32),
         pltpu.VMEM((2, levels, CHUNK, width_y), f32),
-        pltpu.SemaphoreType.DMA((5,)),
-        pltpu.SemaphoreType.DMA((3,)),
+        pltpu.SemaphoreType.DMA((9,)),
+        pltpu.SemaphoreType.DMA((1 + width_x // CHUNK,)),
         pltpu.SemaphoreType.DMA((n_sends,)),
         pltpu.SemaphoreType.DMA((n_sends,)),
     ]
-    return pl.pallas_call(
+    outs = pl.pallas_call(
         functools.partial(kernel, counts),
         out_shape=(
             jax.ShapeDtypeStruct(tracer.shape, f32),
             jax.ShapeDtypeStruct(velocity.shape, f32),
             jax.ShapeDtypeStruct(height.shape, f32),
         ),
-        in_specs=[hbm, hbm, hbm, hbm, vmem, vmem, vmem, vmem, smem, smem],
+        in_specs=[hbm] * 8 + [smem] * 2,
         out_specs=(hbm, hbm, vmem),
         scratch_shapes=scratch,
         compiler_params=pltpu.CompilerParams(
-            collective_id=0, has_side_effects=True, vmem_limit_bytes=40 * 1024 * 1024
+            collective_id=0, has_side_effects=True, vmem_limit_bytes=60 * 1024 * 1024
         ),
         cost_estimate=pl.CostEstimate(
             flops=40 * 3 * levels * width_x * width_y,
             bytes_accessed=8 * 4 * levels * width_x * width_y,
             transcendentals=0,
         ),
-    )(*args)
+    )(*args[:8], args[8].T, args[9].T)
+    return pl.pallas_call(
+        write_out,
+        out_shape=tuple(jax.ShapeDtypeStruct(out.shape, f32) for out in outs),
+        in_specs=[hbm] * 3,
+        out_specs=(hbm,) * 3,
+        scratch_shapes=[pltpu.VMEM(out.shape, f32) for out in outs]
+        + [pltpu.SemaphoreType.DMA((10,))] * 2,
+        compiler_params=pltpu.CompilerParams(vmem_limit_bytes=60 * 1024 * 1024),
+    )(*outs)
 
 
 def solution(mesh):

time: 41.5 us -> 29.5 us (0.71)
  local copies, waits for them, and re-layouts: 14.5 us -> 0 us
  Pallas kernels: 25.9 us -> 28.5 us
    unnamed x21 -> x0, local copies, waits for them, and re-layouts: 14.5 us -> none
    pallas_call x0 -> x1, Pallas kernels: none -> 4.24 us  [shards(): pl.pallas_call(write_out, out_shape=tuple((jax.ShapeDtypeStruct(out.shape...]
    pallas_call x1, Pallas kernels: 25.9 us -> 24.2 us  [shards(): pl.pallas_call(functools.partial(kernel, counts), out_shape=(jax.ShapeDty...]
where the time goes in v2:
time: 29.5 us; the launch traced here: 29.1 us
  Pallas kernels  28.5 us (97%)
  between operations  0.64 us (2%)
    pallas_call x1, Pallas kernels, shards(): pl.pallas_call(functools.partial(kernel, counts), out_shape=(jax.ShapeDty...  24.2 us
    pallas_call x1, Pallas kernels, shards(): pl.pallas_call(write_out, out_shape=tuple((jax.ShapeDtypeStruct(out.shape...  4.24 us

profile of v2, /device:TPU:1, one launch (start us, length us, event | category | flops | bytes accessed | tf_op | source)
XLA Modules:
  0.0 29.1 jit_solution(11751833177867971013)
XLA Ops:
  0.6 24.2 %shard_map.121 = (f32[24,128,128]{2,1,0:T(8,128)}, f32[2,24,128,128]{3,2,1,0:T(8,128)}, f32[1,6,16,128]{3,2,1,0:T(8,128)}) custom-call(f32[24,128,128]{2,1,0:T(8,128)} %tracer.1, f32[2,24,128,128]{3,2,1,0:T(8,128)} %velocity.1, f32[24,128,128]{2,1,0:T(8,128)} %vert_diff.1, f32[24,128,128]{2,1,0:T(8,128)} %vert_visc.1, f32[128,128]{1,0:T(8,128)} %flux_in.1, ...), custom_call_target="tpu_custom_call" | custom-call | flops 47185920 | bytes 12582912 | tf_op jit(solution)/shard_map/pallas_call | solution.py:486
  24.8 4.2 %shard_map.122 = (f32[24,128,128]{2,1,0:T(8,128)}, f32[2,24,128,128]{3,2,1,0:T(8,128)}, f32[1,6,16,128]{3,2,1,0:T(8,128)}) custom-call(f32[24,128,128]{2,1,0:T(8,128)} %get-tuple-element.6.a, f32[2,24,128,128]{3,2,1,0:T(8,128)} %get-tuple-element.7.b, f32[1,6,16,128]{3,2,1,0:T(8,128)} %get-tuple-element.8.c), custom_call_target="tpu_custom_call" | custom-call | tf_op jit(solution)/shard_map/pallas_call | solution.py:505
